TPU v7x, 128 devices: a whole 4x4x4 slice. The times are simulated.
128 devices in a mesh: pipe: 4 (over y_hi, core), fsdp: 32 (over x, z, y_lo).
Axes of the slice: x: 4, y: 4 (y_hi: 2, y_lo: 2; y = y_hi * 2 + y_lo), z: 4, core: 2. Of those that a mesh axis runs over, the one named last changes fastest.
Arguments:
- inputs: bfloat16 [4, 2048, 8192], P(None, 'fsdp'), may hold values from -60 to 60
- cotangent: bfloat16 [4, 2048, 8192], P(None, 'fsdp'), may hold values from -0.25 to 0.25
- right_factor: bfloat16 [4, 64, 128, 128], P('pipe', 'fsdp'), may hold values from -0.5 to 0.5
- left_factor: bfloat16 [4, 64, 128, 128], P('pipe', 'fsdp'), may hold values from -0.5 to 0.5
- norm_gain: bfloat16 [4, 8192], P('pipe', 'fsdp'), may hold values from 0.25 to 1.75
Outputs:
- grad_right: float32 [4, 64, 128, 128], P('pipe', 'fsdp')
- grad_left: float32 [4, 64, 128, 128], P('pipe', 'fsdp')
- grad_gain: float32 [4, 8192], P('pipe', 'fsdp')
All inputs are finite; a program needn't handle non-finite values.
Results may differ from a plain program's by a relative error of at most 0.034.
Values may be sent and summed in bfloat16 or wider, within the bound.
No kernel may reach another device: no remote copies, remote signals or barrier semaphores. Data moves between devices by JAX's collectives and lax.ppermute only.
A program may use at most 192 MiB of HBM per device.

v0:
```python
import jax
import jax.numpy as jnp
from jax import lax
from jax.sharding import PartitionSpec as P

EPSILON = 1e-05
TANH_SLOPE = 0.7978845608028654
CUBIC_TERM = 0.044715


def passed_along(value, axis, by):
    devices = lax.axis_size(axis)
    pairs = [(i, i + by) for i in range(devices) if 0 <= i + by < devices]
    return lax.ppermute(value, axis, pairs)


def gelu_value(pre_act):
    return (
        0.5
        * pre_act
        * (1.0 + jnp.tanh(TANH_SLOPE * (pre_act + CUBIC_TERM * pre_act * pre_act * pre_act)))
    )


def gelu_slope(pre_act):
    inner_tanh = jnp.tanh(TANH_SLOPE * (pre_act + CUBIC_TERM * pre_act * pre_act * pre_act))
    return 0.5 * (1.0 + inner_tanh) + 0.5 * pre_act * (
        1.0 - inner_tanh * inner_tanh
    ) * TANH_SLOPE * (1.0 + 3.0 * CUBIC_TERM * pre_act * pre_act)


def layer_parts(rows_in, gain_row, right_blocks, left_blocks):
    row_count = rows_in.shape[0]
    blocks = right_blocks.shape[0]
    block_size = right_blocks.shape[1]
    share_size = block_size // blocks
    float_in = rows_in.astype(jnp.float32)
    rms_scale = lax.rsqrt(jnp.mean(float_in * float_in, axis=-1, keepdims=True) + EPSILON)
    normed = (float_in * rms_scale * gain_row.astype(jnp.float32)).astype(jnp.bfloat16)
    first_out = jnp.einsum(
        "tkc,kcd->tkd",
        normed.reshape(row_count, blocks, block_size),
        right_blocks,
        preferred_element_type=jnp.float32,
    ).astype(jnp.bfloat16)
    permuted = (
        first_out.reshape(row_count, blocks, share_size, blocks)
        .transpose(0, 3, 1, 2)
        .reshape(row_count, blocks, block_size)
    )
    pre_act = jnp.einsum(
        "tjc,jcd->tjd", permuted, left_blocks, preferred_element_type=jnp.float32
    ).reshape(row_count, blocks * block_size)
    return (float_in, rms_scale, normed, permuted, pre_act)


def layer_forward(rows_in, gain_row, right_blocks, left_blocks):
    parts = layer_parts(rows_in, gain_row, right_blocks, left_blocks)
    return (parts[0] + gelu_value(parts[4])).astype(jnp.bfloat16)


def layer_back(parts, gain_row, right_blocks, left_blocks, grad_out):
    float_in, rms_scale, normed, permuted, pre_act = parts
    row_count = float_in.shape[0]
    blocks = right_blocks.shape[0]
    block_size = right_blocks.shape[1]
    share_size = block_size // blocks
    grad_float = grad_out.astype(jnp.float32)
    grad_pre = (
        (grad_float * gelu_slope(pre_act))
        .astype(jnp.bfloat16)
        .reshape(row_count, blocks, block_size)
    )
    grad_perm = jnp.einsum(
        "tjd,jcd->tjc", grad_pre, left_blocks, preferred_element_type=jnp.float32
    ).astype(jnp.bfloat16)
    grad_first = (
        grad_perm.reshape(row_count, blocks, blocks, share_size)
        .transpose(0, 2, 3, 1)
        .reshape(row_count, blocks, block_size)
    )
    grad_normed = jnp.einsum(
        "tkd,kcd->tkc", grad_first, right_blocks, preferred_element_type=jnp.float32
    ).reshape(row_count, blocks * block_size)
    grad_gain = jnp.sum(grad_normed * float_in * rms_scale, axis=0)
    weighted = grad_normed * gain_row.astype(jnp.float32)
    grad_in = (
        grad_float
        + rms_scale * weighted
        - float_in * rms_scale**3 * jnp.mean(weighted * float_in, axis=-1, keepdims=True)
    ).astype(jnp.bfloat16)
    flat_width = blocks * block_size
    return (
        grad_in,
        normed,
        permuted.reshape(row_count, flat_width),
        grad_pre.reshape(row_count, flat_width),
        grad_first.reshape(row_count, flat_width),
        grad_gain,
    )


def store_slot(buffer_all, new_value, slot_index, is_valid):
    position = (jnp.int32(0), slot_index, jnp.int32(0), jnp.int32(0))
    sizes = (buffer_all.shape[0], 1, buffer_all.shape[2], buffer_all.shape[3])
    old_value = lax.dynamic_slice(buffer_all, position, sizes)
    chosen = jnp.where(is_valid, new_value[:, None], old_value)
    return lax.dynamic_update_slice(buffer_all, chosen, position)


def per_device(inputs, cotangent, right_factor, left_factor, norm_gain):
    segment_count = lax.axis_size("pipe")
    segment_index = lax.axis_index("pipe")
    group_size = 1
    micro_count, token_rows, feature_width = inputs.shape
    group_count = micro_count // group_size
    row_count = group_size * token_rows
    layers = right_factor.shape[0]
    full_right, full_left, full_gain = (
        lax.all_gather(right_factor, "fsdp", axis=1, tiled=True),
        lax.all_gather(left_factor, "fsdp", axis=1, tiled=True),
        lax.all_gather(norm_gain, "fsdp", axis=1, tiled=True),
    )
    step_count = group_count + segment_count - 1
    kept_inputs = jnp.zeros((group_count, row_count, feature_width), jnp.bfloat16)
    carried = jnp.zeros((row_count, feature_width), jnp.bfloat16)
    for time_step in range(step_count):
        micro_index = time_step - segment_index
        is_valid = (micro_index >= 0) & (micro_index < group_count)
        slot_index = jnp.clip(micro_index, 0, group_count - 1)
        segment_in = jnp.where(segment_index == 0, inputs[min(time_step, group_count - 1)], carried)

        def run_forward(activ_rows):
            activ_rows = layer_forward(activ_rows, full_gain[0], full_right[0], full_left[0])
            return activ_rows

        def skip_forward(activ_rows):
            return activ_rows

        result = lax.cond(is_valid, run_forward, skip_forward, segment_in)
        old_rows = lax.dynamic_index_in_dim(kept_inputs, slot_index, 0, keepdims=False)
        kept_inputs = lax.dynamic_update_index_in_dim(
            kept_inputs, jnp.where(is_valid, segment_in, old_rows), slot_index, 0
        )
        if time_step + 1 < step_count:
            carried = passed_along(result, "pipe", 1)
    back_right, back_left, back_gain = (
        lax.all_gather(right_factor, "fsdp", axis=1, tiled=True),
        lax.all_gather(left_factor, "fsdp", axis=1, tiled=True),
        lax.all_gather(norm_gain, "fsdp", axis=1, tiled=True),
    )
    saved_shape = (layers, group_count, row_count, feature_width)
    saved_normed = jnp.zeros(saved_shape, jnp.bfloat16)
    saved_perm = jnp.zeros(saved_shape, jnp.bfloat16)
    saved_pre = jnp.zeros(saved_shape, jnp.bfloat16)
    saved_first = jnp.zeros(saved_shape, jnp.bfloat16)
    gain_total = jnp.zeros((layers, feature_width), jnp.float32)
    carried = jnp.zeros((row_count, feature_width), jnp.bfloat16)
    for time_step in range(step_count):
        micro_index = time_step - (segment_count - 1 - segment_index)
        is_valid = (micro_index >= 0) & (micro_index < group_count)
        slot_index = jnp.clip(micro_index, 0, group_count - 1)
        incoming = jnp.where(
            segment_index == segment_count - 1, cotangent[min(time_step, group_count - 1)], carried
        )
        rows_start = lax.dynamic_index_in_dim(kept_inputs, slot_index, 0, keepdims=False)

        def run_backward(operands):
            rows_now, grad_now = operands
            layer = 0
            parts = layer_parts(rows_now, back_gain[layer], back_right[layer], back_left[layer])
            part_list = [parts]
            normed_list = [None] * layers
            perm_list = [None] * layers
            pre_list = [None] * layers
            first_list = [None] * layers
            gain_list = [None] * layers
            for layer in reversed(range(layers)):
                grad_now, normed, permuted, grad_pre, grad_first, grad_gain = layer_back(
                    part_list[layer],
                    back_gain[layer],
                    back_right[layer],
                    back_left[layer],
                    grad_now,
                )
                normed_list[layer] = normed
                perm_list[layer] = permuted
                pre_list[layer] = grad_pre
                first_list[layer] = grad_first
                gain_list[layer] = grad_gain
            return (
                grad_now,
                jnp.stack(normed_list),
                jnp.stack(perm_list),
                jnp.stack(pre_list),
                jnp.stack(first_list),
                jnp.stack(gain_list),
            )

        def skip_backward(operands):
            empty_rows = jnp.zeros((layers, row_count, feature_width), jnp.bfloat16)
            return (
                operands[1],
                empty_rows,
                empty_rows,
                empty_rows,
                empty_rows,
                jnp.zeros((layers, feature_width), jnp.float32),
            )

        grad_result, step_normed, step_perm, step_pre, step_first, step_gain = lax.cond(
            is_valid, run_backward, skip_backward, (rows_start, incoming)
        )
        saved_normed = store_slot(saved_normed, step_normed, slot_index, is_valid)
        saved_perm = store_slot(saved_perm, step_perm, slot_index, is_valid)
        saved_pre = store_slot(saved_pre, step_pre, slot_index, is_valid)
        saved_first = store_slot(saved_first, step_first, slot_index, is_valid)
        gain_total = gain_total + step_gain
        if time_step + 1 < step_count:
            carried = passed_along(grad_result, "pipe", -1)
    blocks = full_right.shape[1]
    block_size = full_right.shape[2]
    sums_right = jnp.einsum(
        "lmtkc,lmtkd->lkcd",
        saved_normed.reshape(layers, group_count, row_count, blocks, block_size),
        saved_first.reshape(layers, group_count, row_count, blocks, block_size),
        preferred_element_type=jnp.float32,
    )
    sums_left = jnp.einsum(
        "lmtjc,lmtjd->ljcd",
        saved_perm.reshape(layers, group_count, row_count, blocks, block_size),
        saved_pre.reshape(layers, group_count, row_count, blocks, block_size),
        preferred_element_type=jnp.float32,
    )
    total_right, total_left, total_gain = (
        lax.psum_scatter(
            sums_right.astype(jnp.bfloat16), "fsdp", scatter_dimension=1, tiled=True
        ).astype(jnp.float32),
        lax.psum_scatter(
            sums_left.astype(jnp.bfloat16), "fsdp", scatter_dimension=1, tiled=True
        ).astype(jnp.float32),
        lax.psum_scatter(
            gain_total.astype(jnp.bfloat16), "fsdp", scatter_dimension=1, tiled=True
        ).astype(jnp.float32),
    )
    return (total_right, total_left, total_gain)


def solution(mesh):
    return jax.shard_map(
        per_device,
        mesh=mesh,
        in_specs=(
            P(None, "fsdp", None),
            P(None, "fsdp", None),
            P("pipe", "fsdp", None, None),
            P("pipe", "fsdp", None, None),
            P("pipe", "fsdp"),
        ),
        out_specs=(P("pipe", "fsdp", None, None), P("pipe", "fsdp", None, None), P("pipe", "fsdp")),
        check_vma=False,
    )
```

profile of v0, /device:TPU:0, one launch (start us, length us, event | category | flops | bytes accessed | tf_op | source)
XLA Modules:
  0.0 1640.9 jit_solution(37930423273759428)
XLA Ops:
  8.7 82.9 %all_gather.12 = bf16[1,8192]{1,0:T(2,128)(2,1)S(1)} all-gather(bf16[1,256]{1,0:T(2,128)(2,1)} %param.35), channel_id=1, replica_groups=mesh['pipe'=4,'fsdp'=32] {'fsdp'}, dimensions={1}, use_global_device_ids=true | all-gather | bytes 16896 | tf_op jit(solution)/shard_map/all_gather | solution.py:150
  96.6 68.7 %all-gather.3.cloned.1.call-done = bf16[1,64,128,128]{3,2,0,1:T(8,128)(2,1)} async-done(((bf16[1,2,128,128]{3,2,0,1:T(8,128)(2,1)}), bf16[1,64,128,128]{3,2,0,1:T(8,128)(2,1)}) %all-gather.3.cloned.1.call-update) | async-done | bytes 2097168 | tf_op jit(solution)/shard_map/all_gather | solution.py:148
  165.3 155.1 %all-gather.5.cloned.1.call-done = bf16[1,64,128,128]{3,2,0,1:T(8,128)(2,1)} async-done(((bf16[1,2,128,128]{3,2,0,1:T(8,128)(2,1)}), bf16[1,64,128,128]{3,2,0,1:T(8,128)(2,1)}) %all-gather.5.cloned.1.call-update) | async-done | bytes 2097168 | tf_op jit(solution)/shard_map/all_gather | solution.py:149
  320.4 17.8 %conditional.13 = (bf16[64,8192]{1,0:T(8,128)(2,1)S(1)}) conditional(s32[]{:T(128)} %convert_element_type.675, bf16[64,8192]{1,0:T(8,128)(2,1)S(1)} %get-tuple-element.697, (bf16[64,8192]{1,0:T(8,128)(2,1)S(1)}, bf16[1,8192]{1,0:T(2,128)(2,1)S(1)}, bf16[1,64,128,128]{3,2,0,1:T(8,128)(2,1)}, bf16[1,64,128,128]{3,2,0,1:T(8,128)(2,1)}) %tuple.170), branch_computations={%region_0.1_spmd, %region_1.3_spmd} | conditional | flops 278405184 | bytes 29443108 | solution.py:140
  344.7 19.7 %conditional.14 = (bf16[64,8192]{1,0:T(8,128)(2,1)S(1)}) conditional(s32[]{:T(128)} %convert_element_type.676, bf16[64,8192]{1,0:T(8,128)(2,1)S(1)} %get-tuple-element.676, (bf16[64,8192]{1,0:T(8,128)(2,1)S(1)}, bf16[1,8192]{1,0:T(2,128)(2,1)S(1)}, bf16[1,64,128,128]{3,2,0,1:T(8,128)(2,1)S(1)}, bf16[1,64,128,128]{3,2,0,1:T(8,128)(2,1)}) %tuple.296), branch_computations={%region_3.4_spmd, %region_4.6_spmd} | conditional | flops 278405184 | bytes 21054472 | solution.py:140
  372.0 19.7 %conditional.15 = (bf16[64,8192]{1,0:T(8,128)(2,1)S(1)}) conditional(s32[]{:T(128)} %convert_element_type.677, bf16[64,8192]{1,0:T(8,128)(2,1)S(1)} %get-tuple-element.674, (bf16[64,8192]{1,0:T(8,128)(2,1)S(1)}, bf16[1,8192]{1,0:T(2,128)(2,1)S(1)}, bf16[1,64,128,128]{3,2,0,1:T(8,128)(2,1)S(1)}, bf16[1,64,128,128]{3,2,0,1:T(8,128)(2,1)}) %tuple.297), branch_computations={%region_6.7_spmd, %region_7.9_spmd} | conditional | flops 278405184 | bytes 21054472 | solution.py:140
  391.7 13.4 collective-permute-start.2
  409.0 19.4 %conditional.16 = (bf16[64,8192]{1,0:T(8,128)(2,1)S(1)}) conditional(s32[]{:T(128)} %convert_element_type.678, bf16[64,8192]{1,0:T(8,128)(2,1)S(1)} %get-tuple-element.672, (bf16[64,8192]{1,0:T(8,128)(2,1)S(1)}, bf16[1,8192]{1,0:T(2,128)(2,1)S(1)}, bf16[1,64,128,128]{3,2,0,1:T(8,128)(2,1)S(1)}, bf16[1,64,128,128]{3,2,0,1:T(8,128)(2,1)}) %tuple.298), branch_computations={%region_9.10_spmd, %region_10.12_spmd} | conditional | flops 278405184 | bytes 21054472 | solution.py:140
  428.4 16.0 collective-permute-start.3
  448.5 36.0 %collective-permute-start.4 = (bf16[64,8192]{1,0:T(8,128)(2,1)S(1)}, bf16[64,8192]{1,0:T(8,128)(2,1)}, u32[]{:S(2)}, u32[]{:S(2)}) collective-permute-start(bf16[64,8192]{1,0:T(8,128)(2,1)S(1)} %get-tuple-element.789), channel_id=1, source_target_pairs={{0,32},{32,64},{64,96},{1,33},{33,65},{65,97},{2,34},{34,66},{66,9... | collective-permute-start | bytes 3145736 | tf_op jit(solution)/shard_map/ppermute | solution.py:14
  489.0 16.6 %collective-permute-start.5 = (bf16[64,8192]{1,0:T(8,128)(2,1)}, bf16[64,8192]{1,0:T(8,128)(2,1)}, u32[]{:S(2)}, u32[]{:S(2)}) collective-permute-start(bf16[64,8192]{1,0:T(8,128)(2,1)} %get-tuple-element.790), channel_id=1, source_target_pairs={{0,32},{32,64},{64,96},{1,33},{33,65},{65,97},{2,34},{34,66},{66,9... | collective-permute-start | bytes 3145736 | tf_op jit(solution)/shard_map/ppermute | solution.py:14
  512.2 12.4 conditional.19
  533.7 25.4 %collective-permute-done.6 = bf16[64,8192]{1,0:T(8,128)(2,1)S(1)} collective-permute-done((bf16[64,8192]{1,0:T(8,128)(2,1)}, bf16[64,8192]{1,0:T(8,128)(2,1)S(1)}, u32[]{:S(2)}, u32[]{:S(2)}) %collective-permute-start.6) | collective-permute-done | bytes 1048608 | tf_op jit(solution)/shard_map/ppermute | solution.py:14
  576.5 10.4 collective-permute-done.7
  588.3 8.0 conditional.21
  607.5 178.4 %collective-permute-done.8 = bf16[64,8192]{1,0:T(8,128)(2,1)S(1)} collective-permute-done((bf16[64,8192]{1,0:T(8,128)(2,1)S(1)}, bf16[64,8192]{1,0:T(8,128)(2,1)S(1)}, u32[]{:S(2)}, u32[]{:S(2)}) %collective-permute-start.8) | collective-permute-done | bytes 1048608 | tf_op jit(solution)/shard_map/ppermute | solution.py:14
  787.3 75.2 %conditional.22 = (bf16[64,8192]{1,0:T(8,128)(2,1)S(1)}, f32[1,8192]{1,0:T(1,128)S(1)}, bf16[1,1,64,8192]{3,2,1,0:T(8,128)(2,1)}, bf16[1,1,64,8192]{3,2,1,0:T(8,...) conditional(s32[]{:T(128)} %convert_element_type.683, ...), branch_computations={%region_33.34_spmd, %region_34.38_spmd} | conditional | flops 572522688 | bytes 86199688 | solution.py:211
  881.8 75.7 %conditional.23 = (bf16[64,8192]{1,0:T(8,128)(2,1)S(1)}, f32[1,8192]{1,0:T(1,128)S(1)}, bf16[1,1,64,8192]{3,2,1,0:T(8,128)(2,1)}, bf16[1,1,64,8192]{3,2,1,0:T(8,...) conditional(s32[]{:T(128)} %convert_element_type.684, ...), branch_computations={%region_38.39_spmd, %region_39.43_spmd} | conditional | flops 572522688 | bytes 86199688 | solution.py:211
  976.5 75.7 %conditional.24 = (bf16[64,8192]{1,0:T(8,128)(2,1)S(1)}, f32[1,8192]{1,0:T(1,128)S(1)}, bf16[1,1,64,8192]{3,2,1,0:T(8,128)(2,1)}, bf16[1,1,64,8192]{3,2,1,0:T(8,...) conditional(s32[]{:T(128)} %convert_element_type.685, ...), branch_computations={%region_43.44_spmd, %region_44.48_spmd} | conditional | flops 572522688 | bytes 86199688 | solution.py:211
  1070.5 63.1 %conditional.25 = (f32[1,8192]{1,0:T(1,128)S(1)}, bf16[1,1,64,8192]{3,2,1,0:T(8,128)(2,1)}, bf16[1,1,64,8192]{3,2,1,0:T(8,128)(2,1)S(1)}, bf16[1,1,64,8192]{3,2,...) conditional(s32[]{:T(128)} %convert_element_type.686, () %tuple.182, (pred[64,8192]{1,0:T(8,128)(4,1)}, ...), branch_computations={%region_48.49_spmd, %region_49.52_spmd} | conditional | flops 556269632 | bytes 109725552 | solution.py:211
  1147.2 10.2 fusion.489
  1173.2 136.4 %reduce-scatter.10.cloned.1.call-done = bf16[256,1]{1,0:T(8,128)(2,1)} async-done(((bf16[8192,1]{1,0:T(8,128)(2,1)}), bf16[256,1]{1,0:T(8,128)(2,1)}) %reduce-scatter.10.cloned.1.call-update) | async-done | bytes 528
  1311.1 160.3 %reduce-scatter.8.cloned.1.call-done = bf16[1,2,128,128]{3,2,1,0:T(8,128)(2,1)} async-done(((bf16[1,64,128,128]{3,2,1,0:T(8,128)(2,1)}), bf16[1,2,128,128]{3,2,1,0:T(8,128)(2,1)}) %reduce-scatter.8.cloned.1.call-update) | async-done | bytes 65552 | tf_op jit(solution)/shard_map/reduce_scatter | solution.py:239
  1472.9 159.8 %reduce-scatter.6.cloned.1.call-done = bf16[1,2,128,128]{3,2,1,0:T(8,128)(2,1)} async-done(((bf16[1,64,128,128]{3,2,1,0:T(8,128)(2,1)}), bf16[1,2,128,128]{3,2,1,0:T(8,128)(2,1)}) %reduce-scatter.6.cloned.1.call-update) | async-done | bytes 65552 | tf_op jit(solution)/shard_map/reduce_scatter | solution.py:236
  (298 shorter events, 548.0 us)
Async XLA Ops:
  7.2 158.1 %all-gather.3.cloned.1.call-start = ((), (), s32[]{:S(2)}) async-start(), calls=%async_computation.3 | async-start | bytes 2162688 | tf_op jit(solution)/shard_map/all_gather | solution.py:148
  7.9 312.5 %all-gather.5.cloned.1.call-start = ((), (), s32[]{:S(2)}) async-start(), calls=%async_computation.4 | async-start | bytes 2162688 | tf_op jit(solution)/shard_map/all_gather | solution.py:149
  8.6 1301.0 %reduce-scatter.10.cloned.1.call-start = ((), (), s32[]{:S(2)}) async-start(), calls=%async_computation.7 | async-start | bytes 2162688
  329.9 5.4 copy-start.1
  338.2 3.7 collective-permute-start
  364.3 5.0 collective-permute-start.1
  391.7 14.7 collective-permute-start.2
  428.4 17.4 %collective-permute-start.3 = (bf16[64,8192]{1,0:T(8,128)(2,1)S(1)}, bf16[64,8192]{1,0:T(8,128)(2,1)}, u32[]{:S(2)}, u32[]{:S(2)}) collective-permute-start(bf16[64,8192]{1,0:T(8,128)(2,1)S(1)} %get-tuple-element.788), channel_id=1, source_target_pairs={{0,32},{32,64},{64,96},{1,33},{33,65},{65,97},{2,34},{34,66},{66,9... | collective-permute-start | bytes 3145736 | tf_op jit(solution)/shard_map/ppermute | solution.py:14
  448.5 37.4 %collective-permute-start.4 = (bf16[64,8192]{1,0:T(8,128)(2,1)S(1)}, bf16[64,8192]{1,0:T(8,128)(2,1)}, u32[]{:S(2)}, u32[]{:S(2)}) collective-permute-start(bf16[64,8192]{1,0:T(8,128)(2,1)S(1)} %get-tuple-element.789), channel_id=1, source_target_pairs={{0,32},{32,64},{64,96},{1,33},{33,65},{65,97},{2,34},{34,66},{66,9... | collective-permute-start | bytes 3145736 | tf_op jit(solution)/shard_map/ppermute | solution.py:14
  489.0 20.6 %collective-permute-start.5 = (bf16[64,8192]{1,0:T(8,128)(2,1)}, bf16[64,8192]{1,0:T(8,128)(2,1)}, u32[]{:S(2)}, u32[]{:S(2)}) collective-permute-start(bf16[64,8192]{1,0:T(8,128)(2,1)} %get-tuple-element.790), channel_id=1, source_target_pairs={{0,32},{32,64},{64,96},{1,33},{33,65},{65,97},{2,34},{34,66},{66,9... | collective-permute-start | bytes 3145736 | tf_op jit(solution)/shard_map/ppermute | solution.py:14
  524.6 34.5 %collective-permute-start.6 = (bf16[64,8192]{1,0:T(8,128)(2,1)}, bf16[64,8192]{1,0:T(8,128)(2,1)S(1)}, u32[]{:S(2)}, u32[]{:S(2)}) collective-permute-start(bf16[64,8192]{1,0:T(8,128)(2,1)} %get-tuple-element.417), channel_id=1, source_target_pairs={{32,0},{64,32},{96,64},{33,1},{65,33},{97,65},{34,2},{66,34},{98,6... | collective-permute-start | bytes 3145736 | tf_op jit(solution)/shard_map/ppermute | solution.py:14
  533.7 26.8 %copy-start.9 = (bf16[1,4,64,8192]{3,2,1,0:T(8,128)(2,1)}, bf16[1,4,64,8192]{3,2,1,0:T(8,128)(2,1)S(1)}, u32[]{:S(2)}) copy-start(bf16[1,4,64,8192]{3,2,1,0:T(8,128)(2,1)S(1)} %select_dynamic-update-slice_fusion.27) | copy-start | bytes 12582916
  568.5 18.4 %collective-permute-start.7 = (bf16[64,8192]{1,0:T(8,128)(2,1)S(1)}, bf16[64,8192]{1,0:T(8,128)(2,1)S(1)}, u32[]{:S(2)}, u32[]{:S(2)}) collective-permute-start(bf16[64,8192]{1,0:T(8,128)(2,1)S(1)} %get-tuple-element.419), channel_id=1, source_target_pairs={{32,0},{64,32},{96,64},{33,1},{65,33},{97,65},{34,2},{66,34},{98,6... | collective-permute-start | bytes 3145736 | tf_op jit(solution)/shard_map/ppermute | solution.py:14
  596.3 189.7 %collective-permute-start.8 = (bf16[64,8192]{1,0:T(8,128)(2,1)S(1)}, bf16[64,8192]{1,0:T(8,128)(2,1)S(1)}, u32[]{:S(2)}, u32[]{:S(2)}) collective-permute-start(bf16[64,8192]{1,0:T(8,128)(2,1)S(1)} %get-tuple-element.421), channel_id=1, source_target_pairs={{32,0},{64,32},{96,64},{33,1},{65,33},{97,65},{34,2},{66,34},{98,6... | collective-permute-start | bytes 3145736 | tf_op jit(solution)/shard_map/ppermute | solution.py:14
  834.1 5.3 copy-start.20
  862.6 17.9 %collective-permute-start.9 = (bf16[64,8192]{1,0:T(8,128)(2,1)S(1)}, bf16[64,8192]{1,0:T(8,128)(2,1)S(1)}, u32[]{:S(2)}, u32[]{:S(2)}) collective-permute-start(bf16[64,8192]{1,0:T(8,128)(2,1)S(1)} %get-tuple-element.423), channel_id=1, source_target_pairs={{32,0},{64,32},{96,64},{33,1},{65,33},{97,65},{34,2},{66,34},{98,6... | collective-permute-start | bytes 3145736 | tf_op jit(solution)/shard_map/ppermute | solution.py:14
  928.9 5.3 copy-start.21
  957.5 17.6 %collective-permute-start.10 = (bf16[64,8192]{1,0:T(8,128)(2,1)S(1)}, bf16[64,8192]{1,0:T(8,128)(2,1)S(1)}, u32[]{:S(2)}, u32[]{:S(2)}) collective-permute-start(bf16[64,8192]{1,0:T(8,128)(2,1)S(1)} %get-tuple-element.425), channel_id=1, source_target_pairs={{32,0},{64,32},{96,64},{33,1},{65,33},{97,65},{34,2},{66,34},{98,6... | collective-permute-start | bytes 3145736 | tf_op jit(solution)/shard_map/ppermute | solution.py:14
  1023.6 5.3 copy-start.22
  1052.2 17.4 %collective-permute-start.11 = (bf16[64,8192]{1,0:T(8,128)(2,1)S(1)}, bf16[64,8192]{1,0:T(8,128)(2,1)S(1)}, u32[]{:S(2)}, u32[]{:S(2)}) collective-permute-start(bf16[64,8192]{1,0:T(8,128)(2,1)S(1)} %get-tuple-element.427), channel_id=1, source_target_pairs={{32,0},{64,32},{96,64},{33,1},{65,33},{97,65},{34,2},{66,34},{98,6... | collective-permute-start | bytes 3145736 | tf_op jit(solution)/shard_map/ppermute | solution.py:14
  1118.3 6.2 copy-start.15
  1136.1 5.5 copy-start.13
  1147.2 324.3 %reduce-scatter.8.cloned.1.call-start = ((), (), s32[]{:S(2)}) async-start(), calls=%async_computation.6 | async-start | bytes 2162688 | tf_op jit(solution)/shard_map/reduce_scatter | solution.py:239
  1157.4 475.3 %reduce-scatter.6.cloned.1.call-start = ((), (), s32[]{:S(2)}) async-start(), calls=%async_computation.5 | async-start | bytes 2162688 | tf_op jit(solution)/shard_map/reduce_scatter | solution.py:236
  (25 other events, 60.3 us)
Sparse Core Ops, SparseCore 0:
  9.6 155.6 all-gather.2
  166.9 153.4 all-gather.4
  1147.3 162.2 reduce-scatter.9
  1312.0 159.4 reduce-scatter.7
  1473.6 159.0 reduce-scatter.5
where the time goes:
time: 1650 us; the launch traced here: 1640 us
  waiting for transfers between devices  912 us (55%)
  local copies, waits for them, and re-layouts  300 us (18%)
  other arithmetic  135 us (8%)
  starting transfers between devices  95.9 us (6%)
  matrix products  84.3 us (5%)
  blocking collectives  82.9 us (5%)
  loops' own time  17.1 us (1%)
    ppermute x12, waiting for transfers between devices, passed_along(): return lax.ppermute(value, axis, pairs)  230 us
    reduce_scatter x1, waiting for transfers between devices, per_device(): lax.psum_scatter(sums_left.astype(jnp.bfloat16), 'fsdp', scatter_dimensio...  160 us
    reduce_scatter x1, waiting for transfers between devices, per_device(): lax.psum_scatter(sums_right.astype(jnp.bfloat16), 'fsdp', scatter_dimensi...  160 us
    all_gather x1, waiting for transfers between devices, per_device(): lax.all_gather(left_factor, 'fsdp', axis=1, tiled=True)  155 us
    unnamed x6, waiting for transfers between devices  138 us
    ppermute x12, starting transfers between devices, passed_along(): return lax.ppermute(value, axis, pairs)  95.5 us
    all_gather x1, blocking collectives, per_device(): lax.all_gather(norm_gain, 'fsdp', axis=1, tiled=True)  82.9 us
    reshape x16, local copies, waits for them, and re-layouts, layer_parts(): first_out.reshape(row_count, blocks, share_size, blocks)  79.3 us
  transfers between devices with their start and end apart: 17, of which 15 were waited for; matrix products, arithmetic and copies ran while one was open for 6% of the time, Pallas kernels for 0%

commit v1 on v0

v1 whole, which is shorter than its diff:
```python
import functools

import jax
import jax.numpy as jnp
from jax import lax
from jax.experimental import pallas as pl
from jax.experimental.pallas import tpu as pltpu
from jax.sharding import Mesh, PartitionSpec as P

EPSILON = 1e-05
TANH_SLOPE = 0.7978845608028654
CUBIC_TERM = 0.044715

BF = jnp.bfloat16
F32 = jnp.float32
HI = lax.Precision.HIGHEST
SWAP = ((0, 1), (1, 0))
XZ = ("x", "z")
VMEM_LIMIT = 56 * 1024 * 1024

NB = 64
BS = 128
D = NB * BS
HB = NB // 2
ROWS = HB * BS
HALF = ROWS // 2
TOK = 128
STAT = 16
GRID = 4
BPC = HB // GRID


def mm(a, b):
    return lax.dot_general(a, b, (((1,), (0,)), ((), ())), preferred_element_type=F32)


def mm_ta(a, b):
    return lax.dot_general(a, b, (((0,), (0,)), ((), ())), preferred_element_type=F32)


def mm_tb(a, b):
    return lax.dot_general(a, b, (((1,), (1,)), ((), ())), preferred_element_type=F32)


def iota2(dim):
    return lax.broadcasted_iota(jnp.int32, (BS, BS), dim)


def column_source(dp, q):
    rel = dp // 64
    return ((dp // 32) % 2) * 64 + 2 * (dp % 32) + (rel + q - 2 * rel * q)


def row_source(cp, q):
    rel = cp // 64
    return 4 * ((cp % 64) // 2) + 2 * (rel + q - 2 * rel * q) + cp % 2


def stat_rows(value):
    hi = value.astype(BF)
    rest = value - hi.astype(F32)
    mid = rest.astype(BF)
    lo = (rest - mid.astype(F32)).astype(BF)
    row = lax.broadcasted_iota(jnp.int32, (STAT, TOK), 0)
    out = jnp.where(row == 0, hi.astype(F32), jnp.where(row == 1, mid.astype(F32), lo.astype(F32)))
    return jnp.where(row < 3, out, 0.0).astype(BF)


def stat_total(own_ref, recv_ref):
    rows = recv_ref[pl.ds(HALF, STAT), :].astype(F32)
    return own_ref[0:1, :] + jnp.sum(rows, axis=0, keepdims=True)


def folded(value):
    return jnp.sum(value.reshape(BS // 8, 8, TOK), axis=0)


def fold_block(ref, i):
    return ref[i // 2, i % 2]


def prep_kernel(core_ref, right_ref, left_ref, gain_ref, keep_ref, send_ref):
    core = core_ref[0]
    for dst, q in ((keep_ref, core), (send_ref, 1 - core)):
        gain_row = gain_ref[q].astype(F32)
        diag = jnp.where(iota2(0) == iota2(1), gain_row, 0.0).astype(BF)
        scaled = mm(diag, right_ref[q]).astype(BF)
        pick = (iota2(0) == column_source(iota2(1), q)).astype(F32).astype(BF)
        dst[0] = mm(scaled, pick).astype(BF)
        pick = (iota2(1) == row_source(iota2(0), q)).astype(F32).astype(BF)
        dst[1] = mm(pick, left_ref[q]).astype(BF)


def put_forward(scr, pair, product):
    for part in range(2):
        for h in range(2):
            scr[part, pl.ds(pair * 2 + h, 32, stride=64), :] = product[part * 64 + h * 32 :][:32]


def put_backward(scr, pair, product):
    for part in range(2):
        scr[part, pl.ds(pair, 64, stride=32), :] = product[part * 64 :][:64]


def flush(scr, acc, own_ref, send_ref, stat_ref):
    @pl.when(pl.program_id(0) == GRID - 1)
    def _():
        own_ref[...] = scr[0].astype(BF)
        send_ref[pl.ds(0, HALF), :] = scr[1].astype(BF)
        total = jnp.sum(acc[...], axis=0, keepdims=True)
        send_ref[pl.ds(HALF, STAT), :] = stat_rows(total)
        stat_ref[...] = jnp.broadcast_to(total, stat_ref.shape)


def clear(acc):
    @pl.when(pl.program_id(0) == 0)
    def _():
        acc[...] = jnp.zeros_like(acc)


def tokens_last(ref, i, core):
    start = pl.multiple_of((2 * i + core) * BS, BS)
    rows = ref[:, :, pl.ds(start, BS)].reshape(TOK, BS)
    return rows.astype(F32).T


def start_kernel(place_ref, in_ref, w_ref, x_ref, own_ref, send_ref, stat_ref, scr, acc):
    core = place_ref[0]
    clear(acc)
    base = pl.program_id(0) * BPC
    for i in range(BPC):
        x = tokens_last(in_ref, i, core)
        xb = x.astype(BF)
        x_ref[pl.ds(i * BS, BS), :] = xb
        acc[...] += folded(x * x)
        put_forward(scr, base + i, mm_ta(fold_block(w_ref, i), xb))
    flush(scr, acc, own_ref, send_ref, stat_ref)


def gelu_parts(v):
    sq = v * v
    t = jnp.tanh(v * (TANH_SLOPE + (TANH_SLOPE * CUBIC_TERM) * sq))
    half = 0.5 * t + 0.5
    slope = half + (v * (1.0 - t * t)) * (0.5 * TANH_SLOPE + (1.5 * TANH_SLOPE * CUBIC_TERM) * sq)
    return v * half, slope


def rms_of(own_stat, recv_ref):
    return lax.rsqrt(stat_total(own_stat, recv_ref) * (1.0 / D) + EPSILON)


def permuted_block(own_ref, recv_ref, pair, rms):
    start = pl.multiple_of(pair * 64, 64)
    both = jnp.concatenate([own_ref[pl.ds(start, 64), :], recv_ref[pl.ds(start, 64), :]], axis=0)
    if rms is None:
        return both
    return (both.astype(F32) * rms).astype(BF)


def forward_kernel(
    uo_ref, ur_ref, us_ref, x_ref, left_ref, w_ref,
    xn_ref, slope_ref, perm_ref, rms_ref, own_ref, send_ref, stat_ref, scr, acc,
):
    clear(acc)
    base = pl.program_id(0) * BPC
    rms = rms_of(us_ref, ur_ref)
    rms_ref[...] = jnp.broadcast_to(rms, rms_ref.shape)
    for i in range(BPC):
        rows = pl.ds(i * BS, BS)
        perm = permuted_block(uo_ref, ur_ref, base + i, rms)
        perm_ref[rows, :] = perm
        value, slope = gelu_parts(mm_ta(fold_block(left_ref, i), perm))
        slope_ref[rows, :] = slope.astype(BF)
        xb = (x_ref[rows, :].astype(F32) + value).astype(BF)
        xn_ref[rows, :] = xb
        x = xb.astype(F32)
        acc[...] += folded(x * x)
        put_forward(scr, base + i, mm_ta(fold_block(w_ref, i), xb))
    flush(scr, acc, own_ref, send_ref, stat_ref)


def left_backward(grad, slope, perm, left, rms, pair, scr, acc):
    grad_pre = (grad.astype(F32) * slope).astype(BF)
    grad_left = mm_tb(perm, grad_pre).astype(BF)
    grad_perm = mm(left, grad_pre)
    acc[...] += folded(grad_perm * perm.astype(F32))
    put_backward(scr, pair, grad_perm * rms)
    return grad_left


def turn_kernel(
    place_ref, uo_ref, ur_ref, us_ref, cot_ref, left_ref,
    grad_ref, rms_ref, gl_ref, own_ref, send_ref, stat_ref, scr, acc,
):
    core = place_ref[0]
    clear(acc)
    base = pl.program_id(0) * BPC
    rms = rms_of(us_ref, ur_ref)
    rms_ref[...] = jnp.broadcast_to(rms, rms_ref.shape)
    for i in range(BPC):
        perm = permuted_block(uo_ref, ur_ref, base + i, rms)
        left = fold_block(left_ref, i)
        slope = gelu_parts(mm_ta(left, perm))[1]
        grad = tokens_last(cot_ref, i, core).astype(BF)
        grad_ref[pl.ds(i * BS, BS), :] = grad
        gl_ref[i // 2, i % 2] = left_backward(grad, slope, perm, left, rms, base + i, scr, acc)
    flush(scr, acc, own_ref, send_ref, stat_ref)


def backward_kernel(
    buf_ref, go_ref, gr_ref, gs_ref, rms_ref, rms_below_ref, x_ref, grad_ref, slope_ref, perm_ref, w_ref, left_ref,
    new_ref, out_ref, own_ref, send_ref, stat_ref, scr, acc,
):
    del buf_ref
    clear(acc)
    base = pl.program_id(0) * BPC
    rms = rms_ref[0:1, :]
    rms_below = rms_below_ref[0:1, :]
    coef = stat_total(gs_ref, gr_ref) * (rms * rms * (1.0 / D))
    for i in range(BPC):
        rows = pl.ds(i * BS, BS)
        gf = permuted_block(go_ref, gr_ref, base + i, None)
        x = x_ref[rows, :]
        out_ref[i // 2, i % 2, 0] = mm_tb(x, gf).astype(BF)
        grad = grad_ref[rows, :].astype(F32) + mm(fold_block(w_ref, i), gf) - x.astype(F32) * coef
        grad = grad.astype(BF)
        new_ref[rows, :] = grad
        out_ref[i // 2, i % 2, 1] = left_backward(
            grad, slope_ref[rows, :].astype(F32), perm_ref[rows, :], fold_block(left_ref, i), rms_below, base + i, scr, acc
        )
    flush(scr, acc, own_ref, send_ref, stat_ref)


def last_kernel(buf_ref, go_ref, gr_ref, x_ref, out_ref):
    del buf_ref
    base = pl.program_id(0) * BPC
    for i in range(BPC):
        gf = permuted_block(go_ref, gr_ref, base + i, None)
        out_ref[i // 2, i % 2] = mm_tb(x_ref[pl.ds(i * BS, BS), :], gf).astype(BF)


def sum_kernel(core_ref, part_ref, keep_ref, send_ref):
    core = core_ref[0]
    for dst, i in ((keep_ref, core), (send_ref, 1 - core)):
        for side in range(2):
            dst[side] = (part_ref[0, i, side].astype(F32) + part_ref[1, i, side].astype(F32)) + (
                part_ref[2, i, side].astype(F32) + part_ref[3, i, side].astype(F32)
            )


def finish_kernel(core_ref, keep_ref, recv_ref, right_ref, gain_ref, gr_ref, gl_ref, gg_ref):
    core = core_ref[0]
    for src, q in ((keep_ref, core), (recv_ref, 1 - core)):
        pick = (iota2(1) == column_source(iota2(0), q)).astype(F32)
        raw = lax.dot_general(src[0], pick, (((1,), (0,)), ((), ())), precision=HI, preferred_element_type=F32)
        diag = jnp.where(iota2(0) == iota2(1), gain_ref[q].astype(F32), 0.0)
        gr_ref[q] = lax.dot_general(diag, raw, (((1,), (0,)), ((), ())), precision=HI, preferred_element_type=F32)
        weighted = raw * right_ref[q].astype(F32)
        ones = jnp.ones((8, BS), F32)
        gg_ref[q] = lax.dot_general(
            ones, weighted, (((1,), (1,)), ((), ())), precision=HI, preferred_element_type=F32
        )[0:1]
        pick = (iota2(0) == row_source(iota2(1), q)).astype(F32)
        gl_ref[q] = lax.dot_general(pick, src[1], (((1,), (0,)), ((), ())), precision=HI, preferred_element_type=F32)


def full(shape):
    return pl.BlockSpec(shape, lambda g, *_: (0,) * len(shape))


ACT = pl.BlockSpec((BPC * BS, TOK), lambda g, *_: (g, 0))
ANY = pl.BlockSpec(memory_space=pl.ANY)
U_SHAPES = (
    jax.ShapeDtypeStruct((HALF, TOK), BF),
    jax.ShapeDtypeStruct((HALF + STAT, TOK), BF),
    jax.ShapeDtypeStruct((8, TOK), F32),
)
U_SPECS = tuple(full(s.shape) for s in U_SHAPES)
ACT_SHAPE = jax.ShapeDtypeStruct((ROWS, TOK), BF)
STAT_SHAPE = jax.ShapeDtypeStruct((8, TOK), F32)
STAT_SPEC = full((8, TOK))
SCRATCH = [pltpu.VMEM((2, HALF, TOK), F32), pltpu.VMEM((8, TOK), F32)]
PARAMS = pltpu.CompilerParams(vmem_limit_bytes=VMEM_LIMIT)


def weight_spec(layer, side):
    return pl.BlockSpec(
        (None, 4, None, 2, None, None, BS, BS), lambda g, *_: (g, 0, layer // 2, 0, layer % 2, side, 0, 0)
    )


TOKENS_SPEC = pl.BlockSpec((2, 64, D // GRID), lambda g, place: (place[1], 0, g))


def call(kernel, ins, in_specs, out_shapes, out_specs, scratch=(), grid=GRID, prefetch=0, aliases=None):
    return pl.pallas_call(
        kernel,
        out_shape=out_shapes,
        grid_spec=pltpu.PrefetchScalarGridSpec(
            num_scalar_prefetch=prefetch, grid=(grid,), in_specs=in_specs, out_specs=out_specs, scratch_shapes=scratch
        ),
        input_output_aliases=aliases or {},
        compiler_params=PARAMS,
    )(*ins)


def swapped(value):
    return lax.ppermute(value, "c", SWAP)


def per_device(inputs, cotangent, right_factor, left_factor, norm_gain):
    core = lax.axis_index("c")
    place = jnp.stack([core, lax.axis_index("yh")]).astype(jnp.int32)
    right = right_factor[0]
    left = left_factor[0]
    gain = norm_gain.reshape(2, 1, BS)
    pair = jax.ShapeDtypeStruct((2, BS, BS), BF)
    keep, send = call(
        prep_kernel, (place, right, left, gain), [full((2, BS, BS))] * 2 + [full((2, 1, BS))],
        (pair, pair), (full((2, BS, BS)),) * 2, grid=1, prefetch=1,
    )
    recv = swapped(send)
    mine = jnp.stack([jnp.where(core == 0, keep, recv), jnp.where(core == 0, recv, keep)])
    weights = lax.all_gather(mine, ("x", "z", "yh", "yl"), axis=0, tiled=False).reshape(4, 4, 2, 2, 2, 2, BS, BS)

    x0, uo, us, st = call(
        start_kernel, (place, inputs, weights), [TOKENS_SPEC, weight_spec(0, 0)],
        (ACT_SHAPE,) + U_SHAPES, (ACT,) + U_SPECS, SCRATCH, prefetch=1,
    )
    xs, slopes, perms, rmss = [x0], [], [], []
    for layer in range(3):
        xn, slope, perm, rms, uo, us, st = call(
            forward_kernel, (uo, swapped(us), st, xs[-1], weights, weights),
            list((U_SPECS)) + [ACT, weight_spec(layer, 1), weight_spec(layer + 1, 0)],
            (ACT_SHAPE, ACT_SHAPE, ACT_SHAPE, STAT_SHAPE) + U_SHAPES, (ACT, ACT, ACT, STAT_SPEC) + U_SPECS, SCRATCH,
        )
        xs.append(xn)
        slopes.append(slope)
        perms.append(perm)
        rmss.append(rms)
    buf_shape = jax.ShapeDtypeStruct((4, 4, 2, 4, 2, BS, BS), BF)

    def single(slot):
        return pl.BlockSpec((None, 4, 2, None, None, BS, BS), lambda g, *_: (g, 0, 0, 0, slot, 0, 0))

    grad, rms, buf, uo, us, st = call(
        turn_kernel, (place, uo, swapped(us), st, cotangent, weights),
        list(U_SPECS) + [TOKENS_SPEC, weight_spec(3, 1)],
        (ACT_SHAPE, STAT_SHAPE, buf_shape) + U_SHAPES, (ACT, STAT_SPEC, single(1)) + U_SPECS, SCRATCH, prefetch=1,
    )
    rmss.append(rms)
    for layer in (3, 2, 1):
        both = pl.BlockSpec(
            (None, 4, 2, None, 2, BS, BS), functools.partial(lambda n, g, *_: (g, 0, 0, n, 0, 0, 0), layer)
        )
        grad, buf, uo, us, st = call(
            backward_kernel,
            (buf, uo, swapped(us), st, rmss[layer], rmss[layer - 1], xs[layer], grad, slopes[layer - 1], perms[layer - 1],
             weights, weights),
            [ANY] + list(U_SPECS) + [STAT_SPEC] * 2 + [ACT] * 4 + [weight_spec(layer, 0), weight_spec(layer - 1, 1)],
            (ACT_SHAPE, buf_shape) + U_SHAPES, (ACT, both) + U_SPECS, SCRATCH, aliases={0: 1},
        )
    buf = call(
        last_kernel, (buf, uo, swapped(us), xs[0]), [ANY] + list(U_SPECS[:2]) + [ACT],
        buf_shape, single(0), aliases={0: 0},
    )
    part = lax.psum_scatter(buf.reshape(16, 2, 4, 2, BS, BS), XZ, scatter_dimension=0, tiled=True)[0]
    rights = part[:, :, 0]
    lefts = jnp.concatenate([part[:, 1:, 1], part[:, :1, 1]], axis=1)
    piece = jnp.stack([rights, lefts], axis=2).reshape(2, 2, 2, 2, BS, BS).transpose(1, 0, 2, 3, 4, 5)
    piece = lax.all_to_all(piece.reshape(4, 2, 2, BS, BS), ("yh", "yl"), 0, 0, tiled=True)
    sums = jax.ShapeDtypeStruct((2, BS, BS), F32)
    keep, send = call(
        sum_kernel, (place, piece), [full((4, 2, 2, BS, BS))], (sums, sums), (full((2, BS, BS)),) * 2, grid=1, prefetch=1,
    )
    grad_right, grad_left, grad_gain = call(
        finish_kernel, (place, keep, swapped(send), right, gain),
        [full((2, BS, BS))] * 3 + [full((2, 1, BS))],
        (sums, sums, jax.ShapeDtypeStruct((2, 1, BS), F32)),
        (full((2, BS, BS)), full((2, BS, BS)), full((2, 1, BS))), grid=1, prefetch=1,
    )
    return grad_right[None], grad_left[None], grad_gain.reshape(1, 2 * BS)


def solution(mesh):
    parts = Mesh(mesh.devices.reshape(2, 2, 4, 4, 2), ("yh", "c", "x", "z", "yl"))
    pipe, fsdp = ("yh", "c"), ("x", "z", "yl")
    return jax.shard_map(
        per_device,
        mesh=parts,
        in_specs=(P(None, fsdp, None), P(None, fsdp, None), P(pipe, fsdp, None, None), P(pipe, fsdp, None, None), P(pipe, fsdp)),
        out_specs=(P(pipe, fsdp, None, None), P(pipe, fsdp, None, None), P(pipe, fsdp)),
        check_vma=False,
    )
```

time: 1650 us -> 324 us (0.20)
  the two profiles are of different devices: /device:TPU:0 before, /device:TPU:1 now
where the time goes in v1:
time: 324 us; the launch traced here: 323 us
  waiting for transfers between devices  181 us (56%)
  Pallas kernels  85.5 us (26%)
  local copies, waits for them, and re-layouts  20.5 us (6%)
  between operations  14.1 us (4%)
  blocking collectives  10.8 us (3%)
  starting transfers between devices  9.02 us (3%)
    pallas_call x12, Pallas kernels, call(): pl.pallas_call(kernel, out_shape=out_shapes, grid_spec=pltpu.PrefetchScal...  85.5 us
    unnamed x3, waiting for transfers between devices  83.4 us
    all_gather x1, waiting for transfers between devices, per_device(): lax.all_gather(mine, ('x', 'z', 'yh', 'yl'), axis=0, tiled=False)  81 us
    ppermute x10, waiting for transfers between devices, swapped(): return lax.ppermute(value, 'c', SWAP)  16.3 us
    all_to_all x1, blocking collectives, per_device(): lax.all_to_all(piece.reshape(4, 2, 2, BS, BS), ('yh', 'yl'), 0, 0, tiled=...  10.8 us
    reshape x1, local copies, waits for them, and re-layouts, per_device(): buf.reshape(16, 2, 4, 2, BS, BS)  10.4 us
    ppermute x10, starting transfers between devices, swapped(): return lax.ppermute(value, 'c', SWAP)  8.94 us
    unnamed x18, local copies, waits for them, and re-layouts  7.28 us
  transfers between devices with their start and end apart: 12, of which 12 were waited for; matrix products, arithmetic and copies ran while one was open for 0% of the time, Pallas kernels for 0%

profile of v1, /device:TPU:1, one launch (start us, length us, event | category | flops | bytes accessed | tf_op | source)
XLA Modules:
  0.0 322.9 jit_solution(3778835712146840925)
XLA Ops:
  7.8 2.6 shard_map.76
  14.5 81.0 %all-gather.3.cloned.1.call-done = bf16[128,2,128,128]{3,2,1,0:T(8,128)(2,1)} async-done(((bf16[2,2,128,128]{3,2,1,0:T(8,128)(2,1)}), bf16[128,2,128,128]{3,2,1,0:T(8,128)(2,1)}) %all-gather.3.cloned.1.call-update) | async-done | bytes 8388624 | tf_op jit(solution)/shard_map/all_gather | solution.py:324
  95.5 6.2 %shard_map.77 = (bf16[4096,128]{1,0:T(8,128)(2,1)}, bf16[2048,128]{1,0:T(8,128)(2,1)}, bf16[2064,128]{1,0:T(8,128)(2,1)}, f32[8,128]{1,0:T(8,128)}) custom-call(s32[2]{0:T(128)} %pad_add_fusion.core_ref.place_ref, bf16[4,64,8192]{2,1,0:T(8,128)(2,1)} %in_ref.1, bf16[4,4,2,2,2,2,128,128]{7,6,5,4,3,2,1,0:T(8,128)(2,1)} %bitcast.27), custom_call_target="tpu_custom_call" | custom-call | tf_op jit(solution)/shard_map/pallas_call | solution.py:296
  102.5 1.8 collective-permute-done.1.ur_ref
  105.1 7.3 %shard_map.78 = (bf16[4096,128]{1,0:T(8,128)(2,1)}, bf16[4096,128]{1,0:T(8,128)(2,1)}, bf16[4096,128]{1,0:T(8,128)(2,1)}, f32[8,128]{1,0:T(8,128)}, bf16[2048,12...) custom-call(bf16[2048,128]{1,0:T(8,128)(2,1)} %get-tuple-element.56.uo_ref, ...), custom_call_target="tpu_custom_call" | custom-call | tf_op jit(solution)/shard_map/pallas_call | solution.py:296
  115.4 7.3 %shard_map.79 = (bf16[4096,128]{1,0:T(8,128)(2,1)}, bf16[4096,128]{1,0:T(8,128)(2,1)}, bf16[4096,128]{1,0:T(8,128)(2,1)}, f32[8,128]{1,0:T(8,128)}, bf16[2048,12...) custom-call(bf16[2048,128]{1,0:T(8,128)(2,1)} %get-tuple-element.60.uo_ref, ...), custom_call_target="tpu_custom_call" | custom-call | tf_op jit(solution)/shard_map/pallas_call | solution.py:296
  123.2 1.8 collective-permute-done.3.ur_ref
  125.8 7.3 %shard_map.80 = (bf16[4096,128]{1,0:T(8,128)(2,1)}, bf16[4096,128]{1,0:T(8,128)(2,1)}, bf16[4096,128]{1,0:T(8,128)(2,1)}, f32[8,128]{1,0:T(8,128)}, bf16[2048,12...) custom-call(bf16[2048,128]{1,0:T(8,128)(2,1)} %get-tuple-element.64.uo_ref, ...), custom_call_target="tpu_custom_call" | custom-call | tf_op jit(solution)/shard_map/pallas_call | solution.py:296
  133.5 1.8 collective-permute-done.4.ur_ref
  136.1 11.8 %shard_map.81 = (bf16[4096,128]{1,0:T(8,128)(2,1)}, f32[8,128]{1,0:T(8,128)}, bf16[4,4,2,4,2,128,128]{6,5,4,3,2,1,0:T(8,128)(2,1)}, bf16[2048,128]{1,0:T(8,128)(...) custom-call(s32[2]{0:T(128)} %pad_add_fusion.core_ref.place_ref, bf16[2048,128]{1,0:T(8,128)(2,1)} %get-tuple-element.68.uo_ref, ...), custom_call_target="tpu_custom_call" | custom-call | tf_op jit(solution)/shard_map/pallas_call | solution.py:296
  148.3 1.8 collective-permute-done.5.gr_ref
  150.9 11.0 %shard_map.82 = (bf16[4096,128]{1,0:T(8,128)(2,1)}, bf16[4,4,2,4,2,128,128]{6,5,4,3,2,1,0:T(8,128)(2,1)}, bf16[2048,128]{1,0:T(8,128)(2,1)}, bf16[2064,128]{1,0:T(8,128)(2,1)}, f32[8,128]{1,0:T(8,128)}) custom-call(bf16[4,4,2,4,2,128,128]{6,5,4,3,2,1,0:T(8,128)(2,1)} %get-tuple-element.71.buf_ref, ...), custom_call_target="tpu_custom_call", output_to_operand_aliasing={{1}: (0, {})} | custom-call | tf_op jit(solution)/shard_map/pallas_call | solution.py:296
  162.4 1.8 collective-permute-done.6.gr_ref
  165.0 11.0 %shard_map.83 = (bf16[4096,128]{1,0:T(8,128)(2,1)}, bf16[4,4,2,4,2,128,128]{6,5,4,3,2,1,0:T(8,128)(2,1)}, bf16[2048,128]{1,0:T(8,128)(2,1)}, bf16[2064,128]{1,0:T(8,128)(2,1)}, f32[8,128]{1,0:T(8,128)}) custom-call(bf16[4,4,2,4,2,128,128]{6,5,4,3,2,1,0:T(8,128)(2,1)} %get-tuple-element.81.buf_ref, ...), custom_call_target="tpu_custom_call", output_to_operand_aliasing={{1}: (0, {})} | custom-call | tf_op jit(solution)/shard_map/pallas_call | solution.py:296
  176.4 1.8 collective-permute-done.7.gr_ref
  179.0 11.0 %shard_map.84 = (bf16[4096,128]{1,0:T(8,128)(2,1)}, bf16[4,4,2,4,2,128,128]{6,5,4,3,2,1,0:T(8,128)(2,1)}, bf16[2048,128]{1,0:T(8,128)(2,1)}, bf16[2064,128]{1,0:T(8,128)(2,1)}, f32[8,128]{1,0:T(8,128)}) custom-call(bf16[4,4,2,4,2,128,128]{6,5,4,3,2,1,0:T(8,128)(2,1)} %get-tuple-element.89.buf_ref, ...), custom_call_target="tpu_custom_call", output_to_operand_aliasing={{1}: (0, {})} | custom-call | tf_op jit(solution)/shard_map/pallas_call | solution.py:296
  190.7 1.8 collective-permute-done.8.gr_ref
  193.2 4.3 %shard_map.85 = bf16[4,4,2,4,2,128,128]{6,5,4,3,2,1,0:T(8,128)(2,1)} custom-call(bf16[4,4,2,4,2,128,128]{6,5,4,3,2,1,0:T(8,128)(2,1)} %get-tuple-element.97.buf_ref, bf16[2048,128]{1,0:T(8,128)(2,1)} %get-tuple-element.98.go_ref, bf16[2064,128]{1,0:T(8,128)(2,1)} %copy-done.4, bf16[4096,128]{1,0:T(8,128)(2,1)} %get-tuple-element.59.x_ref), custom_call_target="tpu_custom_call", output_to_operand_aliasing={{}: (0, {})} | custom-call | tf_op jit(solution)/shard_map/pallas_call | solution.py:296
  197.5 10.4 %copy.16 = bf16[16,2,4,2,128,128]{5,4,2,1,3,0:T(8,128)(2,1)} copy(bf16[16,2,4,2,128,128]{5,4,3,2,1,0:T(8,128)(2,1)} %bitcast.41) | data formatting | bytes 16777216 | tf_op jit(solution)/shard_map/reshape | solution.py:367
  207.9 83.4 %reduce-scatter.4.cloned.1.call-done = bf16[1,2,4,2,128,128]{5,4,2,1,3,0:T(8,128)(2,1)} async-done(((bf16[16,2,4,2,128,128]{5,4,2,1,3,0:T(8,128)(2,1)}), bf16[1,2,4,2,128,128]{5,4,2,1,3,0:T(8,128)(2,1)}) %reduce-scatter.4.cloned.1.call-update) | async-done | bytes 524304
  294.2 10.8 %all_to_all.5.part_ref = bf16[4,2,2,128,128]{4,3,2,1,0:T(8,128)(2,1)} all-to-all(bf16[4,2,2,128,128]{4,3,2,1,0:T(8,128)(2,1)S(1)} %bitcast.42), channel_id=1, replica_groups=mesh['yh'=2,'c'=2,'x'=4,'z'=4,'yl'=2] {'yh','yl'}, dimensions={0} | all-to-all | bytes 1048576 | tf_op jit(solution)/shard_map/all_to_all | solution.py:371
  305.0 2.4 shard_map.86
  307.5 3.4 %collective-permute-start.9 = (f32[2,128,128]{2,1,0:T(8,128)}, f32[2,128,128]{2,1,0:T(8,128)S(1)}, u32[]{:S(2)}, u32[]{:S(2)}) collective-permute-start(f32[2,128,128]{2,1,0:T(8,128)} %get-tuple-element.101), channel_id=1, source_target_pairs={{0,32},{32,0},{1,33},{33,1},{2,34},{34,2},{3,35},{35,3},{4,36},{36... | collective-permute-start | bytes 393224 | tf_op jit(solution)/shard_map/ppermute | solution.py:308
  312.7 3.3 %shard_map.87 = (f32[2,128,128]{2,1,0:T(8,128)}, f32[2,128,128]{2,1,0:T(8,128)}, f32[2,1,128]{2,1,0:T(1,128)}) custom-call(s32[2]{0:T(128)} %pad_add_fusion.core_ref.place_ref, f32[2,128,128]{2,1,0:T(8,128)} %get-tuple-element.100.keep_ref, f32[2,128,128]{2,1,0:T(8,128)} %copy-done.8, bf16[2,128,128]{2,1,0:T(8,128)(2,1)} %bitcast.49, bf16[2,1,128]{2,1,0:T(2,128)(2,1)} %bitcast.52), custom_call_target="tpu_custom_call" | custom-call | tf_op jit(solution)/shard_map/pallas_call | solution.py:296
  (43 shorter events, 21.9 us)
Async XLA Ops:
  7.2 88.3 %all-gather.3.cloned.1.call-start = ((), (), s32[]{:S(2)}) async-start(), calls=%async_computation.2 | async-start | bytes 8519680 | tf_op jit(solution)/shard_map/all_gather | solution.py:324
  10.4 2.5 collective-permute-start
  14.4 276.8 %reduce-scatter.4.cloned.1.call-start = ((), (), s32[]{:S(2)}) async-start(), calls=%async_computation.3 | async-start | bytes 8912896
  101.7 2.5 collective-permute-start.1
  104.2 0.8 copy-start.5
  112.4 2.2 collective-permute-start.2
  114.6 0.8 copy-start.6
  122.7 2.2 collective-permute-start.3
  124.9 0.8 copy-start.7
  133.1 2.2 collective-permute-start.4
  135.3 0.8 copy-start.3
  147.9 2.2 collective-permute-start.5
  150.1 0.8 copy-start.1
  161.9 2.2 collective-permute-start.6
  164.1 0.9 copy-start.2
  176.0 2.2 collective-permute-start.7
  178.2 0.8 copy-start
  190.0 2.4 collective-permute-start.8
  192.4 0.8 copy-start.4
  307.5 4.6 %collective-permute-start.9 = (f32[2,128,128]{2,1,0:T(8,128)}, f32[2,128,128]{2,1,0:T(8,128)S(1)}, u32[]{:S(2)}, u32[]{:S(2)}) collective-permute-start(f32[2,128,128]{2,1,0:T(8,128)} %get-tuple-element.101), channel_id=1, source_target_pairs={{0,32},{32,0},{1,33},{33,1},{2,34},{34,2},{3,35},{35,3},{4,36},{36... | collective-permute-start | bytes 393224 | tf_op jit(solution)/shard_map/ppermute | solution.py:308
  312.1 0.6 copy-start.8
Sparse Core Ops, SparseCore 0:
  14.6 80.8 all-gather.2
  208.1 83.1 reduce-scatter.3
